TPU v7x, 512 devices: a whole 4x8x8 slice. The times are simulated.
512 devices in a mesh: ctx: 32 (over y, z_lo, core), tp: 16 (over x, z_hi).
Axes of the slice: x: 4, y: 8, z: 8 (z_hi: 4, z_lo: 2; z = z_hi * 2 + z_lo), core: 2. Of those that a mesh axis runs over, the one named last changes fastest.
Arguments:
- quant_codes: bfloat16 [3, 4096, 8192], P(None, 'tp', 'ctx'), may hold values from -127 to 127
- block_scales: bfloat16 [3, 4096, 64], P(None, 'tp', 'ctx'), may hold values from 0.0029907227 to 0.029907227
- conv_taps: float32 [3, 4096, 3], P(None, 'tp'), may hold values from -3 to 3
- decay_rates: float32 [4096, 16], P('tp'), may hold values from 0.00012207031 to 0.05
- residues: float32 [4096, 16], P('tp'), may hold values from -2 to 2
- skip_gain: float32 [4096], P('tp'), may hold values from -4 to 4
- out_weight: bfloat16 [4096, 4096], P('tp'), may hold values from -0.125 to 0.125
Outputs:
- block_output: bfloat16 [4096, 8192], P('tp', 'ctx')
All inputs are finite; a program needn't handle non-finite values.
Results may differ from a plain program's by a relative error of at most 0.015.
Values may be sent and summed in bfloat16 or wider, within the bound.
A program may use at most 64 MiB of HBM per device.

v0:
```python
import math

import jax
import jax.numpy as jnp
from jax import lax
from jax.sharding import PartitionSpec as P

HIGHEST = lax.Precision.HIGHEST


def shifted(block, axis, distance):
    devices = range(lax.axis_size(axis))
    route = [(i - distance, i) for i in devices if i - distance in devices]
    return lax.ppermute(block, axis, route)


def dequantize(codes, scales):
    streams, channels, length = codes.shape
    blocks = scales.shape[2]
    shaped = codes.astype(jnp.float32).reshape(streams, channels, blocks, length // blocks)
    return (shaped * scales.astype(jnp.float32)[:, :, :, None]).reshape(streams, channels, length)


def causal_taps(padded, taps):
    width = taps.shape[-1]
    length = padded.shape[-1] - (width - 1)
    result = jnp.zeros(padded.shape[:2] + (length,), jnp.float32)
    for offset in range(width):
        result = (
            result
            + taps[:, :, offset : offset + 1]
            * padded[:, :, width - 1 - offset : width - 1 - offset + length]
        )
    return result


def with_rim(values, taps):
    width = taps.shape[-1]
    length = values.shape[-1]
    before = shifted(values[:, :, length - (width - 1) :], "ctx", 1)
    return causal_taps(jnp.concatenate([before, values], 2), taps)


def split_sizes(total):
    left_size = 2
    for candidate in range(2, math.isqrt(total) + 1, 2):
        if total % candidate == 0:
            left_size = candidate
    return (left_size, total // left_size)


def dft_tables(left_size, right_size):
    total = left_size * right_size
    k_left = jnp.arange(left_size, dtype=jnp.int32)[:, None]
    n_half = jnp.arange(left_size // 2, dtype=jnp.int32)[None, :]
    n_right = jnp.arange(right_size, dtype=jnp.int32)
    angle_left = 2.0 * math.pi / left_size * (k_left * n_half % left_size).astype(jnp.float32)
    angle_twist = 2.0 * math.pi / total * (k_left * n_right[None, :] % total).astype(jnp.float32)
    angle_right = (
        2.0
        * math.pi
        / right_size
        * (n_right[:, None] * n_right[None, :] % right_size).astype(jnp.float32)
    )
    return (
        jnp.cos(angle_left),
        jnp.sin(angle_left),
        jnp.cos(angle_twist),
        jnp.sin(angle_twist),
        jnp.cos(angle_right),
        jnp.sin(angle_right),
    )


def forward_transform(signal, tables):
    cos_left, sin_left, cos_twist, sin_twist, cos_right, sin_right = tables
    shaped = signal.reshape(signal.shape[0], cos_left.shape[1], cos_right.shape[0])
    first_real = jnp.einsum("kn,cnq->ckq", cos_left, shaped, precision=HIGHEST)
    first_imag = -jnp.einsum("kn,cnq->ckq", sin_left, shaped, precision=HIGHEST)
    twist_real = first_real * cos_twist + first_imag * sin_twist
    twist_imag = first_imag * cos_twist - first_real * sin_twist
    out_real = jnp.einsum("ckq,qm->ckm", twist_real, cos_right, precision=HIGHEST) + jnp.einsum(
        "ckq,qm->ckm", twist_imag, sin_right, precision=HIGHEST
    )
    out_imag = jnp.einsum("ckq,qm->ckm", twist_imag, cos_right, precision=HIGHEST) - jnp.einsum(
        "ckq,qm->ckm", twist_real, sin_right, precision=HIGHEST
    )
    return (out_real, out_imag)


def inverse_transform(spec_real, spec_imag, tables):
    cos_left, sin_left, cos_twist, sin_twist, cos_right, sin_right = tables
    total = cos_twist.shape[0] * cos_twist.shape[1]
    back_real = jnp.einsum("ckm,mq->ckq", spec_real, cos_right, precision=HIGHEST) - jnp.einsum(
        "ckm,mq->ckq", spec_imag, sin_right, precision=HIGHEST
    )
    back_imag = jnp.einsum("ckm,mq->ckq", spec_imag, cos_right, precision=HIGHEST) + jnp.einsum(
        "ckm,mq->ckq", spec_real, sin_right, precision=HIGHEST
    )
    turned_real = back_real * cos_twist - back_imag * sin_twist
    turned_imag = back_imag * cos_twist + back_real * sin_twist
    result = jnp.einsum("kn,ckq->cnq", cos_left, turned_real, precision=HIGHEST) - jnp.einsum(
        "kn,ckq->cnq", sin_left, turned_imag, precision=HIGHEST
    )
    return result.reshape(result.shape[0], -1) / total


def long_convolution(product, rates_here, weights_here, skip_here):
    seq_len = product.shape[1]
    left_size, right_size = split_sizes(2 * seq_len)
    tables = dft_tables(left_size, right_size)
    positions = jnp.arange(seq_len, dtype=jnp.float32)
    impulse = jnp.sum(
        (weights_here * jnp.sqrt(rates_here))[:, :, None]
        * jnp.exp(-rates_here[:, :, None] * positions),
        axis=1,
    )
    signal = product.astype(jnp.float32)
    sig_real, sig_imag = forward_transform(signal, tables)
    imp_real, imp_imag = forward_transform(impulse, tables)
    prod_real = sig_real * imp_real - sig_imag * imp_imag
    prod_imag = sig_real * imp_imag + sig_imag * imp_real
    convolved = inverse_transform(prod_real, prod_imag, tables)
    return (convolved + skip_here[:, None] * signal).astype(jnp.bfloat16)


def on_device(quant_codes, block_scales, conv_taps, decay_rates, residues, skip_gain, out_weight):
    channels = quant_codes.shape[1]
    shards = lax.axis_size("ctx")
    per_device = channels // shards
    offset = lax.axis_index("ctx") * per_device
    filtered = with_rim(dequantize(quant_codes, block_scales), conv_taps)
    product = (filtered[0] * filtered[2]).astype(jnp.bfloat16)
    gate_vals = filtered[1].astype(jnp.bfloat16)
    product_full = lax.all_to_all(product, "ctx", split_axis=0, concat_axis=1, tiled=True)
    rates_here = lax.dynamic_slice_in_dim(decay_rates, offset, per_device, 0)
    weights_here = lax.dynamic_slice_in_dim(residues, offset, per_device, 0)
    skip_here = lax.dynamic_slice_in_dim(skip_gain, offset, per_device, 0)
    long_full = long_convolution(product_full, rates_here, weights_here, skip_here)
    long_conv = lax.all_to_all(long_full, "ctx", split_axis=1, concat_axis=0, tiled=True)
    gated = (gate_vals.astype(jnp.float32) * long_conv.astype(jnp.float32)).astype(jnp.bfloat16)
    summed = lax.psum_scatter(
        lax.dot_general(
            out_weight, gated, (((0,), (0,)), ((), ())), preferred_element_type=jnp.float32
        ),
        "tp",
        scatter_dimension=0,
        tiled=True,
    )
    return summed.astype(jnp.bfloat16)


def solution(mesh):
    return jax.shard_map(
        on_device,
        mesh=mesh,
        in_specs=(
            P(None, "tp", "ctx"),
            P(None, "tp", "ctx"),
            P(None, "tp", None),
            P("tp", None),
            P("tp", None),
            P("tp"),
            P("tp", None),
        ),
        out_specs=P("tp", "ctx"),
        check_vma=False,
    )
```

profile of v0, /device:TPU:1, one launch (start us, length us, event | category | flops | bytes accessed | tf_op | source)
XLA Modules:
  0.0 187.4 jit_solution(1650868432702002759)
XLA Ops:
  6.5 1.0 copy.98
  7.5 1.0 mul.482
  8.5 1.5 mul.483
  10.1 1.3 convert_multiply_fusion
  11.4 0.9 copy-done.1
  12.3 0.9 slice.37
  13.2 5.4 %collective-permute-start = (f32[3,256,2]{2,1,0:T(8,128)}, f32[3,256,2]{2,1,0:T(8,128)}, u32[]{:S(2)}, u32[]{:S(2)}) collective-permute-start(f32[3,256,2]{2,1,0:T(8,128)} %slice.37), channel_id=1, source_target_pairs={{0,16},{16,32},{32,48},{48,64},{64,80},{80,96},{96,112},{112,128},... | collective-permute-start | bytes 18440 | tf_op jit(solution)/shard_map/ppermute | solution.py:14
  18.6 0.3 fusion.82
  18.8 0.3 fusion.81
  19.1 0.1 constant_dynamic-slice_fusion
  19.2 0.1 copy.140
  19.4 1.3 multiply_reduce_fusion
  20.6 1.1 fusion
  21.7 1.1 convolution_bitcast_fusion.1
  22.8 0.1 copy.100
  22.9 0.1 copy.101
  23.0 1.2 fusion.32
  24.2 2.0 %fusion.31 = f32[8,128,128]{2,1,0:T(8,128)} fusion(f32[8,128,128]{1,2,0:T(8,128)S(1)} %fusion, f32[8,128,128]{1,2,0:T(8,128)S(1)} %convolution_bitcast_fusion.1, f32[128,128]{0,1:T(8,128)S(1)} %copy.101, f32[128,128]{0,1:T(8,128)S(1)} %copy.100), kind=kOutput, calls=%fused_computation.56 | convolution fusion | flops 201949184 | bytes 1703936 | tf_op jit(solution)/shard_map/ckq,qm->ckm/dot_general | solution.py:82
  26.2 2.0 %convolution_subtract_fusion.1 = f32[8,128,128]{2,1,0:T(8,128)} fusion(f32[8,128,128]{2,1,0:T(8,128)S(1)} %fusion.32, f32[8,128,128]{1,2,0:T(8,128)S(1)} %fusion, f32[8,128,128]{1,2,0:T(8,128)S(1)} %convolution_bitcast_fusion.1, f32[128,128]{0,1:T(8,128)S(1)} %copy.101, f32[128,128]{0,1:T(8,128)S(1)} %copy.100), kind=kOutput, calls=%fused_computation.10 | convolution fusion | flops 202080256 | bytes 2228224 | tf_op jit(solution)/shard_map/ckq,qm->ckm/dot_general | solution.py:85
  28.2 0.1 dynamic_slice.11
  28.3 2.0 %fusion.7 = f32[3,256,256]{2,1,0:T(8,128)S(1)} fusion(f32[3,256,2]{2,1,0:T(8,128)} %collective-permute-done, f32[3,256,256]{2,1,0:T(8,128)S(1)} %copy-done.2, f32[3,256]{1,0:T(4,128)S(1)} %get-tuple-element.14, f32[3,256]{1,0:T(4,128)S(1)} %get-tuple-element.15, f32[3,256]{1,0:T(4,128)S(1)} %bitcast.89), kind=kLoop, calls=%fused_computation.22 | loop fusion | flops 1376256 | bytes 1588224 | tf_op jit(solution)/shard_map/add | solution.py:30
  30.3 0.9 copy-done.3
  31.2 0.7 fusion.28
  31.9 7.4 %all-to-all-start = ((bf16[32,8,256]{2,1,0:T(8,128)(2,1)}), bf16[32,8,256]{2,1,0:T(8,128)(2,1)S(1)}, u32[]{:S(2)}, u32[]{:S(2)}) async-start(bf16[32,8,256]{2,1,0:T(8,128)(2,1)} %fusion.28), calls=%async_computation | async-start | bytes 262144 | tf_op jit(solution)/shard_map/all_to_all | solution.py:135
  39.3 0.2 reduce-scatter.2.cloned.1.call-start
  39.5 3.0 %convolution_add_fusion.1 = f32[8,128,128]{2,1,0:T(8,128)} fusion(f32[8,128,128]{2,1,0:T(8,128)} %fusion.31, f32[8,128,128]{1,2,0:T(8,128)S(1)} %convolution_bitcast_fusion.1, f32[8,128,128]{1,2,0:T(8,128)S(1)} %fusion, f32[128,128]{0,1:T(8,128)S(1)} %copy.101, f32[128,128]{0,1:T(8,128)S(1)} %copy.100), kind=kOutput, calls=%fused_computation.12 | convolution fusion | flops 202080256 | bytes 2228224 | tf_op jit(solution)/shard_map/ckq,qm->ckm/dot_general | solution.py:82
  42.6 6.0 %all-to-all-done = bf16[32,8,256]{2,1,0:T(8,128)(2,1)S(1)} async-done(((bf16[32,8,256]{2,1,0:T(8,128)(2,1)}), bf16[32,8,256]{2,1,0:T(8,128)(2,1)S(1)}, u32[]{:S(2)}, u32[]{:S(2)}) %all-to-all-start) | async-done | bytes 131104 | tf_op jit(solution)/shard_map/all_to_all | solution.py:135
  48.5 0.7 copy.99
  49.2 1.0 reshape.75
  50.2 0.5 fusion.1
  50.7 0.5 convolution_bitcast_fusion.2
  51.2 1.2 fusion.30
  52.4 1.2 fusion.29
  53.6 1.2 convolution_add_fusion.2
  54.8 1.2 multiply_subtract_fusion
  56.1 0.9 fusion.45
  56.9 0.9 fusion.43
  57.8 0.9 convolution_subtract_fusion
  58.7 0.9 convolution_add_fusion
  59.5 0.9 fusion.12
  60.4 0.9 fusion.3
  61.3 0.1 div.13
  61.4 0.2 fusion.18
  61.6 12.6 %all_to_all.23 = bf16[8,32,256]{2,0,1:T(8,128)(2,1)S(1)} all-to-all(bf16[8,32,256]{2,0,1:T(8,128)(2,1)S(1)} %fusion.18), channel_id=1, replica_groups=mesh['ctx'=32,'tp'=16] {'ctx'}, dimensions={1} | all-to-all | bytes 262144 | tf_op jit(solution)/shard_map/all_to_all | solution.py:140
  74.1 3.6 %convolution_bitcast_fusion = f32[4096,256]{0,1:T(8,128)} fusion(bf16[256,4096]{1,0:T(8,128)(2,1)S(1)} %copy-done, bf16[8,32,256]{2,0,1:T(8,128)(2,1)S(1)} %all_to_all.23, f32[3,256,256]{2,1,0:T(8,128)} %copy-done.3), kind=kOutput, calls=%fused_computation | convolution fusion | flops 537133056 | bytes 6553600 | tf_op jit(solution)/shard_map/dot_general | solution.py:143
  77.8 101.0 %reduce-scatter.2.cloned.1.call-done = f32[256,256]{0,1:T(8,128)} async-done(((f32[4096,256]{0,1:T(8,128)}), f32[256,256]{0,1:T(8,128)}) %reduce-scatter.2.cloned.1.call-update) | async-done | bytes 262160 | tf_op jit(solution)/shard_map/reduce_scatter | solution.py:142
  178.8 1.0 convert_element_type.129
  179.8 0.8 copy.121
  (25 shorter events, 0.1 us)
Async XLA Ops:
  6.5 67.6 %copy-start = (bf16[256,4096]{1,0:T(8,128)(2,1)S(1)}, bf16[256,4096]{1,0:T(8,128)(2,1)}, u32[]{:S(2)}) copy-start(bf16[256,4096]{1,0:T(8,128)(2,1)} %param.13) | copy-start | bytes 6291460
  6.5 12.6 %copy-start.8 = (f32[256,16]{0,1:T(8,128)S(1)}, f32[256,16]{0,1:T(8,128)}, u32[]{:S(2)}) copy-start(f32[256,16]{0,1:T(8,128)} %param.11) | copy-start | bytes 49156
  6.5 12.6 %copy-start.7 = (f32[256,16]{0,1:T(8,128)S(1)}, f32[256,16]{0,1:T(8,128)}, u32[]{:S(2)}) copy-start(f32[256,16]{0,1:T(8,128)} %param.10) | copy-start | bytes 49156
  11.4 0.9 copy-start.1
  12.3 13.9 %copy-start.6 = (f32[3,256,3]{1,2,0:T(4,128)S(1)}, f32[3,256,3]{1,2,0:T(4,128)}, u32[]{:S(2)}) copy-start(f32[3,256,3]{1,2,0:T(4,128)} %param.9) | copy-start | bytes 27652
  13.2 15.1 %collective-permute-start = (f32[3,256,2]{2,1,0:T(8,128)}, f32[3,256,2]{2,1,0:T(8,128)}, u32[]{:S(2)}, u32[]{:S(2)}) collective-permute-start(f32[3,256,2]{2,1,0:T(8,128)} %slice.37), channel_id=1, source_target_pairs={{0,16},{16,32},{32,48},{48,64},{64,80},{80,96},{96,112},{112,128},... | collective-permute-start | bytes 18440 | tf_op jit(solution)/shard_map/ppermute | solution.py:14
  20.6 7.6 %copy-start.9 = (f32[256]{0:T(256)S(1)}, f32[256]{0:T(256)}, u32[]{:S(2)}) copy-start(f32[256]{0:T(256)} %param.12) | copy-start | bytes 3076
  23.0 5.3 %copy-start.2 = (f32[3,256,256]{2,1,0:T(8,128)S(1)}, f32[3,256,256]{2,1,0:T(8,128)}, u32[]{:S(2)}) copy-start(f32[3,256,256]{2,1,0:T(8,128)} %copy-done.1) | copy-start | bytes 2359300
  30.3 0.9 copy-start.3
  31.9 16.6 %all-to-all-start = ((bf16[32,8,256]{2,1,0:T(8,128)(2,1)}), bf16[32,8,256]{2,1,0:T(8,128)(2,1)S(1)}, u32[]{:S(2)}, u32[]{:S(2)}) async-start(bf16[32,8,256]{2,1,0:T(8,128)(2,1)} %fusion.28), calls=%async_computation | async-start | bytes 262144 | tf_op jit(solution)/shard_map/all_to_all | solution.py:135
  39.3 139.5 %reduce-scatter.2.cloned.1.call-start = ((), (), s32[]{:S(2)}) async-start(), calls=%async_computation.3 | async-start | bytes 4456448 | tf_op jit(solution)/shard_map/reduce_scatter | solution.py:142
  42.5 12.3 %copy-start.4 = (f32[8,128,128]{2,1,0:T(8,128)S(1)}, f32[8,128,128]{2,1,0:T(8,128)}, u32[]{:S(2)}) copy-start(f32[8,128,128]{2,1,0:T(8,128)} %convolution_subtract_fusion.1) | copy-start | bytes 1572868
  42.5 12.3 %copy-start.5 = (f32[8,128,128]{2,1,0:T(8,128)S(1)}, f32[8,128,128]{2,1,0:T(8,128)}, u32[]{:S(2)}) copy-start(f32[8,128,128]{2,1,0:T(8,128)} %convolution_add_fusion.1) | copy-start | bytes 1572868
Sparse Core Ops, SparseCore 0:
  77.9 100.8 reduce-scatter.1
where the time goes:
time: 188 us; the launch traced here: 187 us
  waiting for transfers between devices  107 us (57%)
  matrix products  25.1 us (13%)
  between operations  13.7 us (7%)
  starting transfers between devices  13 us (7%)
  blocking collectives  12.6 us (7%)
  local copies, waits for them, and re-layouts  9.17 us (5%)
  other arithmetic  6.91 us (4%)
    reduce_scatter x1, waiting for transfers between devices, on_device(): lax.psum_scatter(lax.dot_general(out_weight, gated, (((0,), (0,)), ((), (...  101 us
    all_to_all x1, blocking collectives, on_device(): lax.all_to_all(long_full, 'ctx', split_axis=1, concat_axis=0, tiled=True)  12.6 us
    all_to_all x1, starting transfers between devices, on_device(): lax.all_to_all(product, 'ctx', split_axis=0, concat_axis=1, tiled=True)  7.37 us
    all_to_all x1, waiting for transfers between devices, on_device(): lax.all_to_all(product, 'ctx', split_axis=0, concat_axis=1, tiled=True)  5.98 us
    ppermute x1, starting transfers between devices, shifted(): return lax.ppermute(block, axis, route)  5.38 us
    dot_general x2, matrix products, forward_transform(): jnp.einsum('ckq,qm->ckm', twist_imag, sin_right, precision=HIGHEST)  4.25 us
  transfers between devices with their start and end apart: 3, of which 2 were waited for; matrix products, arithmetic and copies ran while one was open for 7% of the time, Pallas kernels for 0%

commit v1 on v0

v1 whole, which is shorter than its diff:
```python
import functools

import jax
import jax.numpy as jnp
from jax import lax
from jax.experimental import pallas as pl
from jax.experimental.pallas import tpu as pltpu
from jax.sharding import PartitionSpec as P

MESH = pl.DeviceIdType.MESH
F32 = jnp.float32
BF16 = jnp.bfloat16

Y = 8
Q = 4
X = 4
Z = 4
C = 256
T = 256
O = 256
M = 16
SUB = 8
RUN = T // SUB
LANES = 128
PARTS = 4
ROWS = T // PARTS


def dot(a, b, dims=((1,), (0,))):
    return lax.dot_general(a, b, (dims, ((), ())), preferred_element_type=F32)


def place():
    row = lax.broadcasted_iota(jnp.int32, (T, T), 0)
    col = lax.broadcasted_iota(jnp.int32, (T, T), 1)
    return jnp.where((row % SUB) * RUN + row // SUB == col, 1.0, 0.0).astype(BF16)


def kernel(
    codes_h,
    scales_h,
    taps_h,
    rates_h,
    resid_h,
    skip_h,
    weight_h,
    out_ref,
    codes,
    scales,
    taps,
    rates,
    resid,
    skip,
    wbuf,
    deq,
    prod,
    gate,
    local,
    halo_out,
    halo_in,
    carry,
    decay,
    group_out,
    group_in,
    line_out,
    line_in,
    group_total_coef,
    group_before_coef,
    line_coef,
    entering,
    gown,
    gx,
    held,
    mine,
    opp_out,
    opp_in,
    side_out,
    side_in,
    load_sem,
    halo_sem,
    group_sem,
    line_sem,
    wx_sem,
    wcore_sem,
    wlow_sem,
    wpass_sem,
    gx_sem,
    gpass_sem,
    opp_sem,
    side_sem,
):
    ctx, tp = lax.axis_index("ctx"), lax.axis_index("tp")
    y, q = ctx // Q, ctx % Q
    x, z = tp // Z, tp % Z

    def at_ctx(index):
        return {"ctx": index, "tp": tp}

    def at_tp(index):
        return {"ctx": ctx, "tp": index}

    def group(d):
        return at_ctx(y * Q + q // 2 * 2 + (q + d) % 2 if d == 1 else y * Q + (q + 2) % 4 if d == 2 else y * Q + 3 - q)

    def line(d):
        return at_ctx((y + d) % Y * Q + q)

    def along_x(d):
        return at_tp((x + d) % X * Z + z)

    def along_z(d):
        return at_tp(x * Z + (z + d) % Z)

    def send(src, dst, sems, index, to):
        return pltpu.make_async_remote_copy(
            src_ref=src,
            dst_ref=dst,
            send_sem=sems.at[(0, *index)],
            recv_sem=sems.at[(1, *index)],
            device_id=to,
            device_id_type=MESH,
        )

    following, preceding = at_ctx((ctx + 1) % (Y * Q)), at_ctx((ctx + Y * Q - 1) % (Y * Q))

    barrier = pltpu.get_barrier_semaphore()
    partners = [following, preceding]
    partners += [group(d) for d in (1, 2, 3)]
    partners += [line(d) for d in range(1, Y)]
    partners += [along_x(d) for d in range(1, X)]
    partners += [along_z(d) for d in range(1, Z)]
    for partner in partners:
        pl.semaphore_signal(barrier, inc=1, device_id=partner, device_id_type=MESH)

    loads = [
        pltpu.make_async_copy(src, dst, load_sem.at[i])
        for i, (src, dst) in enumerate(
            [
                (codes_h, codes),
                (scales_h, scales),
                (taps_h, taps),
                (rates_h, rates),
                (resid_h, resid),
                (skip_h, skip),
            ]
        )
    ]
    own_weights = [
        pltpu.make_async_copy(
            weight_h.at[:, pl.ds(pl.multiple_of((x * Z + piece) * O, O), O)],
            wbuf.at[0, piece],
            load_sem.at[6 + piece],
        )
        for piece in range(Z)
    ]
    for load in loads + own_weights:
        load.start()
    for load in loads:
        load.wait()

    order = place()
    run_of = lax.broadcasted_iota(jnp.int32, (SUB, C), 0)
    scale_values = scales[...].astype(F32)
    for s in range(3):
        turned = dot(order, codes[s], ((1,), (1,)))
        scale = jnp.where(run_of < SUB // 2, scale_values[s, 0:1], scale_values[s, 1:2])
        values = (turned.reshape(RUN, SUB, C) * scale[None]).reshape(T, C)
        deq[s, 2 * SUB :, :] = values
        for back in (1, 2):
            last = values[T - back * SUB : T - (back - 1) * SUB]
            halo_out[2 * s + back - 1 : 2 * s + back, :] = last[SUB - 1 : SUB]
            before = jnp.where(run_of == 0, 0.0, pltpu.roll(last, 1, 0))
            deq[s, (2 - back) * SUB : (3 - back) * SUB, :] = before

    def filtered(s, start, rows):
        total = taps[s, 0:1, :] * deq[s, 2 * SUB + start : 2 * SUB + start + rows, :]
        for back in (1, 2):
            first = (2 - back) * SUB + start
            total = total + taps[s, back : back + 1, :] * deq[s, first : first + rows, :]
        return total

    def featurize(start, rows):
        product = (filtered(0, start, rows) * filtered(2, start, rows)).astype(BF16).astype(F32)
        gate[start : start + rows, :] = filtered(1, start, rows).astype(BF16).astype(F32)
        return product

    step = 32
    edge = 2 * SUB
    row16 = lax.broadcasted_iota(jnp.int32, (edge, C), 0)
    prod[0:edge, :] = jnp.where(row16 % SUB == 0, 0.0, featurize(0, edge))
    prod[edge : 2 * edge, :] = featurize(edge, edge)
    for start in range(step, T, step):
        prod[start : start + step, :] = featurize(start, step)

    pl.semaphore_wait(barrier, len(partners))

    halo = send(halo_out, halo_in, halo_sem, (), following)
    halo.start()
    over_x = []
    for d in (1, 3, 2):
        source = weight_h.at[:, pl.ds(pl.multiple_of(((x + d) % X * Z + q) * O, O), O)]
        over_x.append((d, send(source, wbuf.at[d, q], wx_sem, (d - 1,), along_x(d))))
    for _, copy in over_x:
        copy.start()

    a = rates[...]
    for m in range(M):
        decay[m] = jnp.broadcast_to(jnp.exp(-a[m : m + 1]), (SUB, C))
    for lanes in (slice(0, LANES), slice(LANES, C)):
        factor = decay[:, :, lanes]

        def state_step(j, state):
            return state * factor + prod[pl.ds(pl.multiple_of(j * SUB, SUB), SUB), lanes][None]

        carry[:, :, lanes] = lax.fori_loop(0, RUN, state_step, jnp.zeros((M, SUB, LANES), F32), unroll=4)
    for m in range(M):
        state = carry[m]
        rate = a[m : m + 1]
        for reach in (1, 2, 4):
            factor = jnp.where(run_of >= reach, jnp.exp(rate * (-float(reach * RUN))), 0.0)
            state = state + factor * pltpu.roll(state, reach, 0)
        group_out[m : m + 1, :] = state[SUB - 1 : SUB]
        carry[m] = jnp.where(run_of == 0, 0.0, pltpu.roll(state, 1, 0))

    def span(count):
        return jnp.exp(a * (-float(T) * count))

    for d in range(Q):
        source = q if d == 0 else (q // 2 * 2 + (q + 1) % 2 if d == 1 else (q + 2) % 4 if d == 2 else 3 - q)
        group_total_coef[d] = span((Q - 1 - source).astype(F32))
        reach = jnp.maximum(q - 1 - source, 0).astype(F32)
        group_before_coef[d] = jnp.where(source < q, span(reach), 0.0)
    for d in range(1, Y):
        line_coef[d - 1] = span((Q * (d - 1) + q).astype(F32))

    halo.wait()
    first = ctx == 0
    for s in range(3):
        for back in (1, 2):
            row = (2 - back) * SUB
            edge_row = halo_in[2 * s + back - 1 : 2 * s + back, :]
            deq[s, row : row + 1, :] = jnp.where(first, 0.0, edge_row)
    prod[0:edge, :] = featurize(0, edge)
    start0, start1 = prod[0:1, :], prod[SUB : SUB + 1, :]
    group_out[...] = (
        group_out[...] + jnp.exp(a * (1.0 - T)) * start0 + jnp.exp(a * (2.0 - T)) * start1
    )

    in_group = [send(group_out, group_in.at[d - 1], group_sem, (d - 1,), group(d)) for d in (1, 2, 3)]
    for copy in in_group:
        copy.start()

    mix = resid[...] * jnp.sqrt(a)
    for lanes in (slice(0, LANES), slice(LANES, C)):
        factor = decay[:, :, lanes]
        weight = jnp.stack([jnp.broadcast_to(mix[m : m + 1, lanes], (SUB, LANES)) for m in range(M)])

        def local_step(j, state):
            rows = pl.ds(pl.multiple_of(j * SUB, SUB), SUB)
            state = state * factor + prod[rows, lanes][None]
            local[rows, lanes] = jnp.sum(weight * state, axis=0)
            return state

        lax.fori_loop(0, RUN, local_step, jnp.zeros((M, SUB, LANES), F32), unroll=2)

    total = group_total_coef[0] * group_out[...]
    entry = jnp.zeros((M, C), F32)
    for d, copy in zip((1, 2, 3), in_group):
        copy.wait()
        total = total + group_total_coef[d] * group_in[d - 1]
        entry = entry + group_before_coef[d] * group_in[d - 1]
    line_out[...] = total
    entering[...] = entry

    in_line = [send(line_out, line_in.at[d - 1], line_sem, (d - 1,), line(d)) for d in range(1, Y)]
    for d, copy in zip(range(1, Y), in_line):
        pl.when(y + d < Y)(copy.start)

    to_core, to_low, passed = [], [], []
    for d, copy in over_x:
        copy.wait()
        piece = wbuf.at[d, q]
        to_core.append((d, send(piece, piece, wcore_sem, (d - 1,), group(1))))
        to_low.append((d, send(piece, piece, wlow_sem, (d - 1,), group(2))))
        to_low[-1][1].start()
        to_core[-1][1].start()

    for d, copy in zip(range(1, Y), in_line):
        @pl.when(y >= d)
        def _(d=d, copy=copy):
            copy.wait_recv()
            entering[...] = entering[...] + line_coef[d - 1] * line_in[d - 1]

        pl.when(y + d < Y)(copy.wait_send)

    edge_state = jnp.exp(a) * start0 + jnp.exp(a + a) * start1
    enters = entering[...]
    run_number = run_of.astype(F32)
    for m in range(M):
        own = jnp.where(run_of == 0, 0.0, edge_state[m : m + 1])
        reach = jnp.exp(a[m : m + 1] * (-float(RUN) * run_number))
        carry[m] = mix[m : m + 1] * (carry[m] + reach * (enters[m : m + 1] + own))

    gain = skip[...]
    for lanes in (slice(0, LANES), slice(LANES, C)):
        factor = decay[:, :, lanes]

        def join_step(j, state):
            rows = pl.ds(pl.multiple_of(j * 2 * SUB, 2 * SUB), 2 * SUB)
            state = state * factor
            upper = jnp.sum(state, axis=0)
            state = state * factor
            lower = jnp.sum(state, axis=0)
            long = jnp.concatenate([upper, lower], 0) + local[rows, lanes] + gain[:, lanes] * prod[rows, lanes]
            gown[rows, lanes] = (gate[rows, lanes] * long.astype(BF16).astype(F32)).astype(BF16)
            return state

        lax.fori_loop(0, RUN // 2, join_step, carry[:, :, lanes], unroll=2)

    def part(k):
        return pl.ds(k * ROWS, ROWS)

    gathers = []
    for k in range(PARTS):
        right = send(gown.at[part(k)], gx.at[0, part(k)], gx_sem, (0, k), along_x(1))
        left = send(gown.at[part(k)], gx.at[2, part(k)], gx_sem, (1, k), along_x(3))
        right.start()
        left.start()
        gathers.append((right, left))

    for d, copy in to_low:
        copy.wait()
        piece = wbuf.at[d, (q + 2) % 4]
        passed.append((d, send(piece, piece, wpass_sem, (d - 1,), group(1))))
        passed[-1][1].start()
    for d, copy in to_core:
        copy.wait()

    hands = []
    for k in range(PARTS):
        right, left = gathers[k]
        right.wait()
        left.wait()
        source, to = (0, 1) if k % 2 == 0 else (2, 3)
        hands.append(send(gx.at[source, part(k)], gx.at[1, part(k)], gpass_sem, (k,), along_x(to)))
        hands[-1].start()

    for load in own_weights:
        load.wait()
    for _, copy in passed:
        copy.wait()

    def block(k, shift):
        piece = (z + shift) % Z
        rows = part(k)
        result = dot(gown[rows, :], wbuf[0, piece])
        for d in (1, 3, 2):
            result = result + dot(gx[d - 1, rows, :], wbuf[d, piece])
        return result

    opposites, sides = [], []

    def finish(k):
        rows = part(k)
        opposites[k].wait()
        near = 1 if k % 2 == 0 else 3
        slot = 0 if near == 1 else 1
        side_out[slot, rows, :] = (held[rows, :] + opp_in[rows, :].astype(F32)).astype(BF16)
        copy = send(side_out.at[slot, rows], side_in.at[slot, rows], side_sem, (slot, k), along_z(near))
        copy.start()
        sides.append(copy)

    for k in range(PARTS):
        rows = part(k)
        hands[k].wait()
        near, far = (1, 3) if k % 2 == 0 else (3, 1)
        opp_out[rows, :] = block(k, 2).astype(BF16)
        copy = send(opp_out.at[rows], opp_in.at[rows], opp_sem, (k,), along_z(near))
        copy.start()
        opposites.append(copy)
        slot = 0 if far == 1 else 1
        side_out[slot, rows, :] = block(k, far).astype(BF16)
        copy = send(side_out.at[slot, rows], side_in.at[slot, rows], side_sem, (slot, k), along_z(far))
        copy.start()
        sides.append(copy)
        held[rows, :] = block(k, near)
        mine[rows, :] = block(k, 0)
        if k > 0:
            finish(k - 1)
    finish(PARTS - 1)
    for copy in sides:
        copy.wait()

    summed = mine[...] + side_in[0].astype(F32) + side_in[1].astype(F32)
    eye = jnp.where(
        lax.broadcasted_iota(jnp.int32, (O, O), 0) == lax.broadcasted_iota(jnp.int32, (O, O), 1), 1.0, 0.0
    ).astype(BF16)
    features = dot(eye, summed.astype(BF16), ((1,), (1,))).astype(BF16)
    out_ref[...] = dot(features, order).astype(BF16)


def on_device(quant_codes, block_scales, conv_taps, decay_rates, residues, skip_gain, out_weight):
    def vmem(shape, kind=F32):
        return pltpu.VMEM(shape, kind)

    dma = pltpu.SemaphoreType.DMA
    return pl.pallas_call(
        kernel,
        out_shape=jax.ShapeDtypeStruct((O, T), BF16),
        in_specs=[pl.BlockSpec(memory_space=pltpu.HBM)] * 7,
        out_specs=pl.BlockSpec(memory_space=pltpu.VMEM),
        scratch_shapes=[
            vmem((3, C, T), BF16),
            vmem((3, 2, C), BF16),
            vmem((3, 3, C)),
            vmem((M, C)),
            vmem((M, C)),
            vmem((1, C)),
            vmem((X, Z, C, O), BF16),
            vmem((3, T + 2 * SUB, C)),
            vmem((T, C)),
            vmem((T, C)),
            vmem((T, C)),
            vmem((SUB, C)),
            vmem((SUB, C)),
            vmem((M, SUB, C)),
            vmem((M, SUB, C)),
            vmem((M, C)),
            vmem((Q - 1, M, C)),
            vmem((M, C)),
            vmem((Y - 1, M, C)),
            vmem((Q, M, C)),
            vmem((Q, M, C)),
            vmem((Y - 1, M, C)),
            vmem((M, C)),
            vmem((T, C), BF16),
            vmem((X - 1, T, C), BF16),
            vmem((T, O)),
            vmem((T, O)),
            vmem((T, O), BF16),
            vmem((T, O), BF16),
            vmem((2, T, O), BF16),
            vmem((2, T, O), BF16),
            dma((6 + Z,)),
            dma((2,)),
            dma((2, Q - 1)),
            dma((2, Y - 1)),
            dma((2, X - 1)),
            dma((2, X - 1)),
            dma((2, X - 1)),
            dma((2, X - 1)),
            dma((2, 2, PARTS)),
            dma((2, PARTS)),
            dma((2, PARTS)),
            dma((2, 2, PARTS)),
        ],
        compiler_params=pltpu.CompilerParams(
            collective_id=0, has_side_effects=True, vmem_limit_bytes=60 * 1024 * 1024
        ),
        name="hyena",
    )(
        quant_codes,
        jnp.swapaxes(block_scales, 1, 2),
        jnp.swapaxes(conv_taps, 1, 2),
        decay_rates.T,
        residues.T,
        skip_gain.reshape(1, C),
        out_weight,
    )


def solution(mesh):
    return jax.shard_map(
        on_device,
        mesh=mesh,
        in_specs=(
            P(None, "tp", "ctx"),
            P(None, "tp", "ctx"),
            P(None, "tp", None),
            P("tp", None),
            P("tp", None),
            P("tp"),
            P("tp", None),
        ),
        out_specs=P("tp", "ctx"),
        check_vma=False,
    )
```

time: 188 us -> 52.4 us (0.28)
  the two profiles are of different devices: /device:TPU:1 before, /device:TPU:8 now
where the time goes in v1:
time: 52.4 us; the launch traced here: 52.2 us
  Pallas kernels  50.7 us (97%)
  local copies, waits for them, and re-layouts  1.57 us (3%)
    pallas_call x1, Pallas kernels, on_device(): pl.pallas_call(kernel, out_shape=jax.ShapeDtypeStruct((O, T), BF16), in_s...  50.7 us
    unnamed x1, local copies, waits for them, and re-layouts  1.57 us

profile of v1, /device:TPU:8, one launch (start us, length us, event | category | flops | bytes accessed | tf_op | source)
XLA Modules:
  0.0 52.2 jit_solution(1828059294209820378)
XLA Ops:
  0.0 50.7 %hyena.1 = bf16[256,256]{1,0:T(8,128)(2,1)} custom-call(bf16[3,256,256]{2,1,0:T(8,128)(2,1)} %codes_h.1, bf16[3,2,256]{2,1,0:T(2,128)(2,1)} %bitcast.8, f32[3,3,256]{2,1,0:T(4,128)} %bitcast.7, f32[16,256]{1,0:T(8,128)} %bitcast.5, f32[16,256]{1,0:T(8,128)} %bitcast.6, f32[1,256]{1,0:T(1,128)} %bitcast.9, bf16[256,4096]{1,0:T(8,128)(2,1)} %weight_h.1), custom_call_target="tpu_custom_call" | custom-call | tf_op jit(solution)/shard_map/hyena/pallas_call | solution.py:407
  50.7 1.6 %copy.9 = bf16[256,256]{1,0:T(8,128)(2,1)} copy(bf16[256,256]{1,0:T(8,128)(2,1)} %hyena.1) | data formatting | bytes 262144

commit v2 on v1

v2 whole, which is shorter than its diff:
```python
import functools

import jax
import jax.numpy as jnp
from jax import lax
from jax.experimental import pallas as pl
from jax.experimental.pallas import tpu as pltpu
from jax.sharding import PartitionSpec as P

MESH = pl.DeviceIdType.MESH
F32 = jnp.float32
BF16 = jnp.bfloat16

Y = 8
Q = 4
X = 4
Z = 4
C = 256
T = 256
O = 256
M = 16
SUB = 8
RUN = T // SUB
LANES = 128
FIRST = M
LAST = FIRST + 4
EDGED = LAST + 4
PARTS = 4
ROWS = T // PARTS


def dot(a, b, dims=((1,), (0,))):
    return lax.dot_general(a, b, (dims, ((), ())), preferred_element_type=F32)


def place():
    row = lax.broadcasted_iota(jnp.int32, (T, T), 0)
    col = lax.broadcasted_iota(jnp.int32, (T, T), 1)
    return jnp.where((row % SUB) * RUN + row // SUB == col, 1.0, 0.0).astype(BF16)


def kernel(
    codes_h,
    scales_h,
    taps_h,
    rates_h,
    resid_h,
    skip_h,
    weight_h,
    out_ref,
    codes,
    scales,
    taps,
    rates,
    resid,
    skip,
    wbuf,
    deq,
    prod,
    gate,
    local,
    halo_out,
    halo_in,
    carry,
    decay,
    reach_table,
    group_in,
    line_in,
    edge_in,
    gown,
    gx,
    mine,
    sum_out,
    sum_in,
    load_sem,
    halo_sem,
    group_sem,
    edge_sem,
    line_sem,
    wx_sem,
    wcore_sem,
    wpair_sem,
    wpass_sem,
    gx_sem,
    sum_sem,
):
    ctx, tp = lax.axis_index("ctx"), lax.axis_index("tp")
    y, q = ctx // Q, ctx % Q
    x, z = tp // Z, tp % Z

    def at_ctx(index):
        return {"ctx": index, "tp": tp}

    def at_tp(index):
        return {"ctx": ctx, "tp": index}

    def group(d):
        return at_ctx(y * Q + q // 2 * 2 + (q + d) % 2 if d == 1 else y * Q + (q + 2) % 4 if d == 2 else y * Q + 3 - q)

    def line(d):
        return at_ctx((y + d) % Y * Q + q)

    def along_x(d):
        return at_tp((x + d) % X * Z + z)

    def along_z(d):
        return at_tp(x * Z + (z + d) % Z)

    def send(src, dst, sems, index, to):
        return pltpu.make_async_remote_copy(
            src_ref=src,
            dst_ref=dst,
            send_sem=sems.at[(0, *index)],
            recv_sem=sems.at[(1, *index)],
            device_id=to,
            device_id_type=MESH,
        )

    following, preceding = at_ctx((ctx + 1) % (Y * Q)), at_ctx((ctx + Y * Q - 1) % (Y * Q))

    codes_load = pltpu.make_async_copy(codes_h, codes, load_sem.at[0])
    small = [(scales_h, scales), (taps_h, taps), (rates_h, rates), (resid_h, resid), (skip_h, skip)]
    loads = [pltpu.make_async_copy(src, dst, load_sem.at[1 + i]) for i, (src, dst) in enumerate(small)]
    own_weights = [
        pltpu.make_async_copy(
            weight_h.at[:, pl.ds(pl.multiple_of((x * Z + piece) * O, O), O)],
            wbuf.at[0, piece],
            load_sem.at[6 + piece],
        )
        for piece in range(Z)
    ]
    for load in [codes_load] + loads:
        load.start()

    barrier = pltpu.get_barrier_semaphore()
    partners = [following, preceding]
    partners += [group(d) for d in (1, 2, 3)]
    partners += [line(d) for d in range(1, Y)]
    partners += [along_x(d) for d in range(1, X)]
    partners += [along_z(d) for d in range(1, Z)]
    for partner in partners:
        pl.semaphore_signal(barrier, inc=1, device_id=partner, device_id_type=MESH)
    group_before = (y + Y - 1) % Y * Q + Q - 1
    pl.semaphore_signal(barrier, inc=1, device_id=at_ctx(group_before), device_id_type=MESH)
    for load in own_weights:
        load.start()

    order = place()
    run_of = lax.broadcasted_iota(jnp.int32, (SUB, C), 0)
    for load in loads:
        load.wait()
    a = rates[...]
    fall = jnp.exp(-a)
    for m in range(M):
        decay[m] = jnp.broadcast_to(fall[m : m + 1], (SUB, C))
    fall_run = jnp.exp(a * (-float(RUN)))
    fall_own = jnp.exp(a * (-float(T)))
    from_first, from_second = jnp.exp(a * (1.0 - T)), jnp.exp(a * (2.0 - T))
    scale_values = scales[...].astype(F32)
    codes_load.wait()

    def dequantize(s):
        turned = dot(order, codes[s], ((1,), (1,)))
        scale = jnp.where(run_of < SUB // 2, scale_values[s, 0:1], scale_values[s, 1:2])
        values = (turned.reshape(RUN, SUB, C) * scale[None]).reshape(T, C)
        deq[s, 2 * SUB :, :] = values
        for back in (1, 2):
            last = values[T - back * SUB : T - (back - 1) * SUB]
            before = jnp.where(run_of == 0, 0.0, pltpu.roll(last, 1, 0))
            deq[s, (2 - back) * SUB : (3 - back) * SUB, :] = before

    def last_row(s, back):
        row = 2 * SUB + T - back * SUB + SUB - 1
        return deq[s, row : row + 1, :]

    def filtered(s, start, rows):
        total = taps[s, 0:1, :] * deq[s, 2 * SUB + start : 2 * SUB + start + rows, :]
        for back in (1, 2):
            first = (2 - back) * SUB + start
            total = total + taps[s, back : back + 1, :] * deq[s, first : first + rows, :]
        return total

    def products(start, rows):
        return (filtered(0, start, rows) * filtered(2, start, rows)).astype(BF16).astype(F32)

    dequantize(0)
    dequantize(2)
    step = 32
    edge = 2 * SUB
    row16 = lax.broadcasted_iota(jnp.int32, (edge, C), 0)
    prod[0:edge, :] = jnp.where(row16 % SUB == 0, 0.0, products(0, edge))
    prod[edge : 2 * edge, :] = products(edge, edge)
    for start in range(step, T, step):
        prod[start : start + step, :] = products(start, step)

    for lanes in (slice(0, LANES), slice(LANES, C)):
        factor = decay[:, :, lanes]

        def state_step(j, state):
            return state * factor + prod[pl.ds(pl.multiple_of(j * SUB, SUB), SUB), lanes][None]

        carry[:, :, lanes] = lax.fori_loop(0, RUN, state_step, jnp.zeros((M, SUB, LANES), F32), unroll=4)
    mine_in_group = group_in.at[q]
    for m in range(M):
        state = carry[m]
        power = fall_run[m : m + 1]
        for reach in (1, 2, 4):
            state = state + power * jnp.where(run_of >= reach, pltpu.roll(state, reach, 0), 0.0)
            power = power * power
        mine_in_group[m : m + 1, :] = state[SUB - 1 : SUB]
        carry[m] = jnp.where(run_of == 0, 0.0, pltpu.roll(state, 1, 0))
    for n, s in enumerate((0, 2)):
        for row in (0, 1):
            first = 2 * SUB + row * SUB
            mine_in_group[FIRST + 2 * n + row : FIRST + 2 * n + row + 1, :] = deq[s, first : first + 1, :]
            mine_in_group[LAST + 2 * n + row : LAST + 2 * n + row + 1, :] = last_row(s, 2 - row)

    pl.semaphore_wait(barrier, len(partners) + jnp.where(q == Q - 1, Q, 0))

    in_group = [send(mine_in_group, mine_in_group, group_sem, (d - 1,), group(d)) for d in (1, 2, 3)]
    to_next = [
        send(mine_in_group.at[FIRST:EDGED], edge_in, edge_sem, (j,), at_ctx((y + 1) % Y * Q + j)) for j in range(Q)
    ]
    for copy in in_group:
        copy.start()
    for copy in to_next:
        pl.when(q == Q - 1)(copy.start)

    quarters = (q, y % 2 * Q // 2 + q % 2)
    pair = (group(2), at_ctx((y // 2 * 2 + (y + 1) % 2) * Q + q))
    units = [(1, 0, 0, C), (3, 1, 0, C), (2, 0, 0, C // 2), (2, 1, C // 2, C // 2)]
    over_x = []
    for u, (d, way, start, rows) in enumerate(units):
        column = pl.multiple_of(((x + d) % X * Z + quarters[way]) * O, O)
        source = weight_h.at[pl.ds(start, rows), pl.ds(column, O)]
        over_x.append(send(source, wbuf.at[d, quarters[way], pl.ds(start, rows)], wx_sem, (u,), along_x(d)))
    for copy in over_x:
        copy.start()

    dequantize(1)
    for s in range(3):
        for back in (1, 2):
            halo_out[2 * s + back - 1 : 2 * s + back, :] = last_row(s, back)
    halo = send(halo_out, halo_in, halo_sem, (), following)
    halo.start()

    def first_terms(firsts, lasts):
        sides = []
        for n, s in enumerate((0, 2)):
            t0, t1, t2 = (taps[s, j : j + 1, :] for j in range(3))
            x0, x1 = firsts[2 * n : 2 * n + 1], firsts[2 * n + 1 : 2 * n + 2]
            b2, b1 = lasts[2 * n : 2 * n + 1], lasts[2 * n + 1 : 2 * n + 2]
            sides.append((t0 * x0 + t1 * b1 + t2 * b2, t0 * x1 + t1 * x0 + t2 * b1))
        p0, p1 = ((sides[0][i] * sides[1][i]).astype(BF16).astype(F32) for i in (0, 1))
        return from_first * p0 + from_second * p1

    for copy in in_group:
        copy.wait()
    for j in range(Q):
        pl.when(q == j)(to_next[j].wait_recv)
    total = jnp.zeros((M, C), F32)
    entry = jnp.zeros((M, C), F32)
    for source in range(Q):
        if source > 0:
            lasts = group_in[source - 1, LAST:EDGED, :]
        else:
            lasts = jnp.where(y == 0, 0.0, edge_in[LAST - FIRST :, :])
        state = group_in[source, 0:M, :] + first_terms(group_in[source, FIRST:LAST, :], lasts)
        entry = jnp.where(source < q, entry * fall_own + state, entry)
        total = total * fall_own + state
    line_in[y] = total

    mine_in_line = line_in.at[y]
    in_line = [send(mine_in_line, mine_in_line, line_sem, (d - 1,), line(d)) for d in range(1, Y)]
    for d, copy in zip(range(1, Y), in_line):
        pl.when(y + d < Y)(copy.start)

    halo.wait()
    first = ctx == 0
    for s in range(3):
        for back in (1, 2):
            row = (2 - back) * SUB
            edge_row = halo_in[2 * s + back - 1 : 2 * s + back, :]
            deq[s, row : row + 1, :] = jnp.where(first, 0.0, edge_row)
    prod[0:edge, :] = products(0, edge)
    for start in range(0, T, step):
        gate[start : start + step, :] = filtered(1, start, step).astype(BF16).astype(F32)
    mix = resid[...] * jnp.sqrt(a)
    for lanes in (slice(0, LANES), slice(LANES, C)):
        factor = decay[:, :, lanes]
        weight = jnp.stack([jnp.broadcast_to(mix[m : m + 1, lanes], (SUB, LANES)) for m in range(M)])

        def local_step(j, state):
            rows = pl.ds(pl.multiple_of(j * SUB, SUB), SUB)
            state = state * factor + prod[rows, lanes][None]
            local[rows, lanes] = jnp.sum(weight * state, axis=0)
            return state

        lax.fori_loop(0, RUN, local_step, jnp.zeros((M, SUB, LANES), F32), unroll=2)

    to_core, to_pair, passed = [], [], []
    for u, (d, way, start, rows) in enumerate(units):
        over_x[u].wait()
        piece = wbuf.at[d, quarters[way], pl.ds(start, rows)]
        to_pair.append(send(piece, piece, wpair_sem, (u,), pair[way]))
        to_core.append(send(piece, piece, wcore_sem, (u,), group(1)))
        to_pair[u].start()
        to_core[u].start()

    start0, start1 = prod[0:1, :], prod[SUB : SUB + 1, :]
    edge_state = jnp.exp(a) * start0 + jnp.exp(a + a) * start1
    run_number = run_of.astype(F32)
    for m in range(M):
        reaches = mix[m : m + 1] * jnp.exp(a[m : m + 1] * (-float(RUN) * run_number))
        reach_table[m] = reaches
        own = jnp.where(run_of == 0, 0.0, edge_state[m : m + 1])
        carry[m] = mix[m : m + 1] * carry[m] + reaches * own
    fall_group = jnp.exp(a * (-float(Q * T)))
    fall_entry = jnp.exp(a * (-float(T) * q.astype(F32)))

    for d, copy in zip(range(1, Y), in_line):
        pl.when(y >= d)(copy.wait_recv)
    enters = jnp.zeros((M, C), F32)
    for source in range(Y - 1):
        enters = jnp.where(source < y, enters * fall_group + line_in[source], enters)
    enters = enters * fall_entry + entry

    for m in range(M):
        carry[m] = carry[m] + reach_table[m] * enters[m : m + 1]

    gain = skip[...]
    for lanes in (slice(0, LANES), slice(LANES, C)):
        factor = decay[:, :, lanes]

        def join_step(j, state):
            rows = pl.ds(pl.multiple_of(j * 2 * SUB, 2 * SUB), 2 * SUB)
            state = state * factor
            upper = jnp.sum(state, axis=0)
            state = state * factor
            lower = jnp.sum(state, axis=0)
            long = jnp.concatenate([upper, lower], 0) + local[rows, lanes] + gain[:, lanes] * prod[rows, lanes]
            gown[rows, lanes] = (gate[rows, lanes] * long.astype(BF16).astype(F32)).astype(BF16)
            return state

        lax.fori_loop(0, RUN // 2, join_step, carry[:, :, lanes], unroll=2)

    for d, copy in zip(range(1, Y), in_line):
        pl.when(y + d < Y)(copy.wait_send)
    for copy in to_next:
        pl.when(q == Q - 1)(copy.wait_send)

    def part(k):
        return pl.ds(k * ROWS, ROWS)

    gathers = []
    for k in range(PARTS):
        gathers.append([send(gown.at[part(k)], gx.at[d - 1, part(k)], gx_sem, (d - 1, k), along_x(d)) for d in (2, 1, 3)])
        for copy in gathers[k]:
            copy.start()

    for u, (d, way, start, rows) in enumerate(units):
        to_pair[u].wait()
        piece = wbuf.at[d, (quarters[way] + 2) % Q, pl.ds(start, rows)]
        passed.append(send(piece, piece, wpass_sem, (u,), group(1)))
        passed[u].start()
    for load in own_weights:
        load.wait()
    for copy in to_core + passed:
        copy.wait()

    def block(k, piece):
        rows = part(k)
        result = dot(gown[rows, :], wbuf[0, piece])
        for d in (1, 3, 2):
            result = result + dot(gx[d - 1, rows, :], wbuf[d, piece])
        return result

    def message(k, to):
        slot = (to - z + Z - 1) % Z
        return send(sum_out.at[to, part(k)], sum_in.at[slot, part(k)], sum_sem, (slot, k), at_tp(x * Z + to))

    def work(k, to):
        rows = part(k)

        @pl.when(z == to)
        def _():
            mine[rows, :] = block(k, to)

        @pl.when(z != to)
        def _():
            sum_out[to, rows, :] = block(k, to).astype(BF16)
            message(k, to).start()

    for pieces in ((0, 2), (1, 3)):
        for k in range(PARTS):
            if pieces[0] == 0:
                for copy in gathers[k]:
                    copy.wait()
            for to in pieces:
                work(k, to)
    for k in range(PARTS):
        for to in range(Z):
            pl.when(z != to)(message(k, to).wait_send)
    for k in range(PARTS):
        rows = part(k)
        total = mine[rows, :]
        for shift in (1, 2, 3):
            here = send(sum_out.at[0, rows], sum_in.at[shift - 1, rows], sum_sem, (shift - 1, k), along_z(1))
            here.wait_recv()
            total = total + sum_in[shift - 1, rows, :].astype(F32)
        out_ref[rows, :] = total.astype(BF16)


def turn_kernel(rows_ref, out_ref):
    out_ref[...] = dot(rows_ref[...], place(), ((0,), (0,))).astype(BF16)


def on_device(quant_codes, block_scales, conv_taps, decay_rates, residues, skip_gain, out_weight):
    def vmem(shape, kind=F32):
        return pltpu.VMEM(shape, kind)

    dma = pltpu.SemaphoreType.DMA
    rows = pl.pallas_call(
        kernel,
        out_shape=jax.ShapeDtypeStruct((T, O), BF16),
        in_specs=[pl.BlockSpec(memory_space=pltpu.HBM)] * 7,
        out_specs=pl.BlockSpec(memory_space=pltpu.VMEM),
        scratch_shapes=[
            vmem((3, C, T), BF16),
            vmem((3, 2, C), BF16),
            vmem((3, 3, C)),
            vmem((M, C)),
            vmem((M, C)),
            vmem((1, C)),
            vmem((X, Z, C, O), BF16),
            vmem((3, T + 2 * SUB, C)),
            vmem((T, C)),
            vmem((T, C)),
            vmem((T, C)),
            vmem((SUB, C)),
            vmem((SUB, C)),
            vmem((M, SUB, C)),
            vmem((M, SUB, C)),
            vmem((M, SUB, C)),
            vmem((Q, EDGED, C)),
            vmem((Y, M, C)),
            vmem((EDGED - FIRST, C)),
            vmem((T, C), BF16),
            vmem((X - 1, T, C), BF16),
            vmem((T, O)),
            vmem((Z, T, O), BF16),
            vmem((Z - 1, T, O), BF16),
            dma((6 + Z,)),
            dma((2,)),
            dma((2, Q - 1)),
            dma((2, Q)),
            dma((2, Y - 1)),
            dma((2, 4)),
            dma((2, 4)),
            dma((2, 4)),
            dma((2, 4)),
            dma((2, X - 1, PARTS)),
            dma((2, Z - 1, PARTS)),
        ],
        compiler_params=pltpu.CompilerParams(
            collective_id=0, has_side_effects=True, vmem_limit_bytes=60 * 1024 * 1024
        ),
        name="hyena",
    )(
        quant_codes,
        jnp.swapaxes(block_scales, 1, 2),
        jnp.swapaxes(conv_taps, 1, 2),
        decay_rates.T,
        residues.T,
        skip_gain.reshape(1, C),
        out_weight,
    )
    return pl.pallas_call(
        turn_kernel,
        out_shape=jax.ShapeDtypeStruct((O, T), BF16),
        compiler_params=pltpu.CompilerParams(vmem_limit_bytes=60 * 1024 * 1024),
        name="turn",
    )(rows)


def solution(mesh):
    return jax.shard_map(
        on_device,
        mesh=mesh,
        in_specs=(
            P(None, "tp", "ctx"),
            P(None, "tp", "ctx"),
            P(None, "tp", None),
            P("tp", None),
            P("tp", None),
            P("tp"),
            P("tp", None),
        ),
        out_specs=P("tp", "ctx"),
        check_vma=False,
    )
```

time: 52.4 us -> 43.6 us (0.83)
  the two profiles are of different devices: /device:TPU:8 before, /device:TPU:129 now
where the time goes in v2:
time: 43.6 us; the launch traced here: 43.4 us
  Pallas kernels  43.4 us (100%)
    pallas_call x1, Pallas kernels, on_device(): pl.pallas_call(kernel, out_shape=jax.ShapeDtypeStruct((T, O), BF16), in_s...  41.7 us
    pallas_call x1, Pallas kernels, on_device(): pl.pallas_call(turn_kernel, out_shape=jax.ShapeDtypeStruct((O, T), BF16),...  1.79 us

profile of v2, /device:TPU:129, one launch (start us, length us, event | category | flops | bytes accessed | tf_op | source)
XLA Modules:
  0.0 43.4 jit_solution(4970543052456899006)
XLA Ops:
  0.0 41.7 %hyena.1.rows_ref = bf16[256,256]{1,0:T(8,128)(2,1)} custom-call(bf16[3,256,256]{2,1,0:T(8,128)(2,1)} %codes_h.1, bf16[3,2,256]{2,1,0:T(2,128)(2,1)} %bitcast.8, f32[3,3,256]{2,1,0:T(4,128)} %bitcast.7, f32[16,256]{1,0:T(8,128)} %bitcast.5, f32[16,256]{1,0:T(8,128)} %bitcast.6, f32[1,256]{1,0:T(1,128)} %bitcast.9, bf16[256,4096]{1,0:T(8,128)(2,1)} %weight_h.1), custom_call_target="tpu_custom_call" | custom-call | tf_op jit(solution)/shard_map/hyena/pallas_call | solution.py:423
  41.7 1.8 %turn.1 = bf16[256,256]{1,0:T(8,128)(2,1)} custom-call(bf16[256,256]{1,0:T(8,128)(2,1)} %hyena.1.rows_ref), custom_call_target="tpu_custom_call" | custom-call | tf_op jit(solution)/shard_map/turn/pallas_call | solution.py:478

commit v3 on v2

--- a/solution.py
+++ b/solution.py
@@ -54,7 +54,8 @@
     rates,
     resid,
     skip,
-    wbuf,
+    wown,
+    wfar,
     deq,
     prod,
     gate,
@@ -78,9 +79,8 @@
     edge_sem,
     line_sem,
     wx_sem,
+    wnear_sem,
     wcore_sem,
-    wpair_sem,
-    wpass_sem,
     gx_sem,
     sum_sem,
 ):
@@ -124,7 +124,7 @@
     own_weights = [
         pltpu.make_async_copy(
             weight_h.at[:, pl.ds(pl.multiple_of((x * Z + piece) * O, O), O)],
-            wbuf.at[0, piece],
+            wown.at[piece],
             load_sem.at[6 + piece],
         )
         for piece in range(Z)
@@ -192,6 +192,17 @@
     prod[edge : 2 * edge, :] = products(edge, edge)
     for start in range(step, T, step):
         prod[start : start + step, :] = products(start, step)
+
+    pl.semaphore_wait(barrier, len(partners) + jnp.where(q == Q - 1, Q, 0))
+
+    colour, core = (y + q // 2 * 2) % Z, q % 2
+    over_x = []
+    for d in (1, 3, 2):
+        column = pl.multiple_of(((x + d) % X * Z + colour) * O, O)
+        source = weight_h.at[pl.ds(pl.multiple_of(core * (C // 2), C // 2), C // 2), pl.ds(column, O)]
+        over_x.append(send(source, wfar.at[colour, core, d - 1], wx_sem, (d - 1,), along_x(d)))
+    for copy in over_x:
+        copy.start()
 
     for lanes in (slice(0, LANES), slice(LANES, C)):
         factor = decay[:, :, lanes]
@@ -215,8 +226,6 @@
             mine_in_group[FIRST + 2 * n + row : FIRST + 2 * n + row + 1, :] = deq[s, first : first + 1, :]
             mine_in_group[LAST + 2 * n + row : LAST + 2 * n + row + 1, :] = last_row(s, 2 - row)
 
-    pl.semaphore_wait(barrier, len(partners) + jnp.where(q == Q - 1, Q, 0))
-
     in_group = [send(mine_in_group, mine_in_group, group_sem, (d - 1,), group(d)) for d in (1, 2, 3)]
     to_next = [
         send(mine_in_group.at[FIRST:EDGED], edge_in, edge_sem, (j,), at_ctx((y + 1) % Y * Q + j)) for j in range(Q)
@@ -225,17 +234,6 @@
         copy.start()
     for copy in to_next:
         pl.when(q == Q - 1)(copy.start)
-
-    quarters = (q, y % 2 * Q // 2 + q % 2)
-    pair = (group(2), at_ctx((y // 2 * 2 + (y + 1) % 2) * Q + q))
-    units = [(1, 0, 0, C), (3, 1, 0, C), (2, 0, 0, C // 2), (2, 1, C // 2, C // 2)]
-    over_x = []
-    for u, (d, way, start, rows) in enumerate(units):
-        column = pl.multiple_of(((x + d) % X * Z + quarters[way]) * O, O)
-        source = weight_h.at[pl.ds(start, rows), pl.ds(column, O)]
-        over_x.append(send(source, wbuf.at[d, quarters[way], pl.ds(start, rows)], wx_sem, (u,), along_x(d)))
-    for copy in over_x:
-        copy.start()
 
     dequantize(1)
     for s in range(3):
@@ -275,6 +273,17 @@
     for d, copy in zip(range(1, Y), in_line):
         pl.when(y + d < Y)(copy.start)
 
+    ways = ((group(2), 2), (line(1), Z - 1), (line(Y - 1), 1))
+    spread, to_core = [], []
+    for d, copy in zip((1, 3, 2), over_x):
+        copy.wait()
+        piece = wfar.at[colour, core, d - 1]
+        for i, (to, _) in enumerate(ways):
+            spread.append(send(piece, piece, wnear_sem, (i, d - 1), to))
+        to_core.append(send(piece, piece, wcore_sem, (len(ways), d - 1), group(1)))
+        for copy in spread[-len(ways) :] + to_core[-1:]:
+            copy.start()
+
     halo.wait()
     first = ctx == 0
     for s in range(3):
@@ -298,15 +307,6 @@
 
         lax.fori_loop(0, RUN, local_step, jnp.zeros((M, SUB, LANES), F32), unroll=2)
 
-    to_core, to_pair, passed = [], [], []
-    for u, (d, way, start, rows) in enumerate(units):
-        over_x[u].wait()
-        piece = wbuf.at[d, quarters[way], pl.ds(start, rows)]
-        to_pair.append(send(piece, piece, wpair_sem, (u,), pair[way]))
-        to_core.append(send(piece, piece, wcore_sem, (u,), group(1)))
-        to_pair[u].start()
-        to_core[u].start()
-
     start0, start1 = prod[0:1, :], prod[SUB : SUB + 1, :]
     edge_state = jnp.exp(a) * start0 + jnp.exp(a + a) * start1
     run_number = run_of.astype(F32)
@@ -358,21 +358,23 @@
         for copy in gathers[k]:
             copy.start()
 
-    for u, (d, way, start, rows) in enumerate(units):
-        to_pair[u].wait()
-        piece = wbuf.at[d, (quarters[way] + 2) % Q, pl.ds(start, rows)]
-        passed.append(send(piece, piece, wpass_sem, (u,), group(1)))
-        passed[u].start()
+    for n, d in enumerate((1, 3, 2)):
+        for i, (_, ahead) in enumerate(ways):
+            spread[n * len(ways) + i].wait()
+            arrived = wfar.at[(colour + ahead) % Z, core, d - 1]
+            to_core.append(send(arrived, arrived, wcore_sem, (i, d - 1), group(1)))
+            to_core[-1].start()
     for load in own_weights:
         load.wait()
-    for copy in to_core + passed:
+    for copy in to_core:
         copy.wait()
 
     def block(k, piece):
         rows = part(k)
-        result = dot(gown[rows, :], wbuf[0, piece])
+        result = dot(gown[rows, :], wown[piece])
         for d in (1, 3, 2):
-            result = result + dot(gx[d - 1, rows, :], wbuf[d, piece])
+            weights = jnp.concatenate([wfar[piece, 0, d - 1], wfar[piece, 1, d - 1]], 0)
+            result = result + dot(gx[d - 1, rows, :], weights)
         return result
 
     def message(k, to):
@@ -432,7 +434,8 @@
             vmem((M, C)),
             vmem((M, C)),
             vmem((1, C)),
-            vmem((X, Z, C, O), BF16),
+            vmem((Z, C, O), BF16),
+            vmem((Z, 2, X - 1, C // 2, O), BF16),
             vmem((3, T + 2 * SUB, C)),
             vmem((T, C)),
             vmem((T, C)),
@@ -455,10 +458,9 @@
             dma((2, Q - 1)),
             dma((2, Q)),
             dma((2, Y - 1)),
-            dma((2, 4)),
-            dma((2, 4)),
-            dma((2, 4)),
-            dma((2, 4)),
+            dma((2, X - 1)),
+            dma((2, 3, X - 1)),
+            dma((2, 4, X - 1)),
             dma((2, X - 1, PARTS)),
             dma((2, Z - 1, PARTS)),
         ],

time: 43.6 us -> 43.2 us (level)
  the two profiles are of different devices: /device:TPU:129 before, /device:TPU:1 now
where the time goes in v3:
time: 43.2 us; the launch traced here: 43.1 us
  Pallas kernels  43.1 us (100%)
    pallas_call x1, Pallas kernels, on_device(): pl.pallas_call(kernel, out_shape=jax.ShapeDtypeStruct((T, O), BF16), in_s...  41.3 us
    pallas_call x1, Pallas kernels, on_device(): pl.pallas_call(turn_kernel, out_shape=jax.ShapeDtypeStruct((O, T), BF16),...  1.79 us

profile of v3, /device:TPU:1, one launch (start us, length us, event | category | flops | bytes accessed | tf_op | source)
XLA Modules:
  0.0 43.1 jit_solution(8627232558318000073)
XLA Ops:
  0.0 41.3 %hyena.1.rows_ref = bf16[256,256]{1,0:T(8,128)(2,1)} custom-call(bf16[3,256,256]{2,1,0:T(8,128)(2,1)} %codes_h.1, bf16[3,2,256]{2,1,0:T(2,128)(2,1)} %bitcast.8, f32[3,3,256]{2,1,0:T(4,128)} %bitcast.7, f32[16,256]{1,0:T(8,128)} %bitcast.5, f32[16,256]{1,0:T(8,128)} %bitcast.6, f32[1,256]{1,0:T(1,128)} %bitcast.9, bf16[256,4096]{1,0:T(8,128)(2,1)} %weight_h.1), custom_call_target="tpu_custom_call" | custom-call | tf_op jit(solution)/shard_map/hyena/pallas_call | solution.py:425
  41.3 1.8 %turn.1 = bf16[256,256]{1,0:T(8,128)(2,1)} custom-call(bf16[256,256]{1,0:T(8,128)(2,1)} %hyena.1.rows_ref), custom_call_target="tpu_custom_call" | custom-call | tf_op jit(solution)/shard_map/turn/pallas_call | solution.py:480

commit v4 on v3

--- a/solution.py
+++ b/solution.py
@@ -201,8 +201,6 @@
         column = pl.multiple_of(((x + d) % X * Z + colour) * O, O)
         source = weight_h.at[pl.ds(pl.multiple_of(core * (C // 2), C // 2), C // 2), pl.ds(column, O)]
         over_x.append(send(source, wfar.at[colour, core, d - 1], wx_sem, (d - 1,), along_x(d)))
-    for copy in over_x:
-        copy.start()
 
     for lanes in (slice(0, LANES), slice(LANES, C)):
         factor = decay[:, :, lanes]
@@ -235,6 +233,9 @@
     for copy in to_next:
         pl.when(q == Q - 1)(copy.start)
 
+    for copy in over_x:
+        copy.start()
+
     dequantize(1)
     for s in range(3):
         for back in (1, 2):
@@ -270,8 +271,8 @@
 
     mine_in_line = line_in.at[y]
     in_line = [send(mine_in_line, mine_in_line, line_sem, (d - 1,), line(d)) for d in range(1, Y)]
-    for d, copy in zip(range(1, Y), in_line):
-        pl.when(y + d < Y)(copy.start)
+    for d in sorted(range(1, Y), key=lambda d: -min(d, Y - d)):
+        pl.when(y + d < Y)(in_line[d - 1].start)
 
     ways = ((group(2), 2), (line(1), Z - 1), (line(Y - 1), 1))
     spread, to_core = [], []
@@ -354,7 +355,7 @@
 
     gathers = []
     for k in range(PARTS):
-        gathers.append([send(gown.at[part(k)], gx.at[d - 1, part(k)], gx_sem, (d - 1, k), along_x(d)) for d in (2, 1, 3)])
+        gathers.append([send(gown.at[part(k)], gx.at[d - 1, part(k)], gx_sem, (d - 1, k), along_x(d)) for d in (1, 3, 2)])
         for copy in gathers[k]:
             copy.start()
 

time: 43.2 us -> 43.4 us (level)
  no operation moved by 1% of the time
where the time goes in v4:
time: 43.4 us; the launch traced here: 43.2 us
  Pallas kernels  43.2 us (100%)
    pallas_call x1, Pallas kernels, on_device(): pl.pallas_call(kernel, out_shape=jax.ShapeDtypeStruct((T, O), BF16), in_s...  41.5 us
    pallas_call x1, Pallas kernels, on_device(): pl.pallas_call(turn_kernel, out_shape=jax.ShapeDtypeStruct((O, T), BF16),...  1.79 us

profile of v4, /device:TPU:1, one launch (start us, length us, event | category | flops | bytes accessed | tf_op | source)
XLA Modules:
  0.0 43.2 jit_solution(11025701431119463945)
XLA Ops:
  0.0 41.5 %hyena.1.rows_ref = bf16[256,256]{1,0:T(8,128)(2,1)} custom-call(bf16[3,256,256]{2,1,0:T(8,128)(2,1)} %codes_h.1, bf16[3,2,256]{2,1,0:T(2,128)(2,1)} %bitcast.8, f32[3,3,256]{2,1,0:T(4,128)} %bitcast.7, f32[16,256]{1,0:T(8,128)} %bitcast.5, f32[16,256]{1,0:T(8,128)} %bitcast.6, f32[1,256]{1,0:T(1,128)} %bitcast.9, bf16[256,4096]{1,0:T(8,128)(2,1)} %weight_h.1), custom_call_target="tpu_custom_call" | custom-call | tf_op jit(solution)/shard_map/hyena/pallas_call | solution.py:426
  41.5 1.8 %turn.1 = bf16[256,256]{1,0:T(8,128)(2,1)} custom-call(bf16[256,256]{1,0:T(8,128)(2,1)} %hyena.1.rows_ref), custom_call_target="tpu_custom_call" | custom-call | tf_op jit(solution)/shard_map/turn/pallas_call | solution.py:481
